TPU v7x, 1024 devices: a whole 4x4x32 slice. The times are simulated.
1024 devices in a mesh: dp: 128 (over y, z_lo, core), mp: 8 (over x, z_hi).
Axes of the slice: x: 4, y: 4, z: 32 (z_hi: 2, z_lo: 16; z = z_hi * 16 + z_lo), core: 2. Of those that a mesh axis runs over, the one named last changes fastest.
Arguments:
- attn: bfloat16 [24576, 3072], P('dp', 'mp'), may hold values from -6 to 6
- w_out: bfloat16 [5120, 3072], P(None, 'mp'), may hold values from -0.109375 to 0.109375
- encoder: bfloat16 [40, 128, 16], replicated, may hold values from -0.5 to 0.5
- decoder: bfloat16 [40, 16, 128], replicated, may hold values from -1.5 to 1.5
- cotangent: bfloat16 [24576, 5120], P('dp'), may hold values from -24 to 24
Outputs:
- mixed: bfloat16 [24576, 5120], P('dp', 'mp')
- grad_attn: bfloat16 [24576, 3072], P('dp', 'mp')
- grad_w: float32 [5120, 3072], P('dp', 'mp')
All inputs are finite; a program needn't handle non-finite values.
Results may differ from a plain program's by a relative error of at most 0.0049.
Values sent between devices are 32-bit elements; how exact they have to be, the bound alone decides.
A program may use at most 64 MiB of HBM per device.

v0:
```python
import jax
import jax.numpy as jnp
from jax import lax
from jax.sharding import PartitionSpec as P


def shards(attn, w_out, encoder, decoder, cotangent):
    high = lax.Precision.HIGHEST
    tok_rows = attn.shape[0]
    width = w_out.shape[0]
    groups = encoder.shape[0]
    group_width = encoder.shape[1]
    mp_count = lax.axis_size("mp")
    dp_count = lax.axis_size("dp")
    own_groups = groups // mp_count
    enc_float = encoder.astype(jnp.float32)
    scale = float(tok_rows * dp_count) ** (-0.5)
    part = jnp.einsum("tr,dr->td", attn, w_out, preferred_element_type=jnp.float32)
    code = jnp.einsum(
        "tgh,ghc->tgc", part.reshape(tok_rows, groups, group_width), enc_float, precision=high
    )
    first_group = lax.axis_index("mp") * own_groups
    own_decoder = lax.dynamic_slice_in_dim(decoder, first_group, own_groups, 0).astype(jnp.float32)
    own_code = lax.psum_scatter(code, "mp", scatter_dimension=1, tiled=True)
    mixed = jnp.einsum("tgc,gch->tgh", own_code, own_decoder, precision=high)
    mixed = mixed.reshape(tok_rows, own_groups * group_width).astype(jnp.bfloat16)
    coded = jnp.einsum(
        "tgh,gch->tgc",
        cotangent.reshape(tok_rows, groups, group_width),
        decoder,
        preferred_element_type=jnp.float32,
    )
    spread = jnp.einsum("tgc,ghc->tgh", coded, enc_float, precision=high).reshape(tok_rows, width)
    grad_attn = jnp.dot(
        spread.astype(jnp.bfloat16), w_out, preferred_element_type=jnp.float32
    ).astype(jnp.bfloat16)
    attn_float = attn.astype(jnp.float32)
    grad_w = lax.psum_scatter(
        jnp.dot(spread.T, attn_float, precision=high) * scale, "dp", scatter_dimension=0, tiled=True
    )
    return (mixed, grad_attn, grad_w)


def solution(mesh):
    placed = (P("dp", "mp"), P(None, "mp"), P(), P(), P("dp", None))
    return jax.shard_map(
        shards,
        mesh=mesh,
        in_specs=placed,
        out_specs=(P("dp", "mp"), P("dp", "mp"), P("dp", "mp")),
        check_vma=False,
    )
```

profile of v0, /device:TPU:7, one launch (start us, length us, event | category | flops | bytes accessed | tf_op | source)
XLA Modules:
  0.0 1665.3 jit_solution(3039285542408762809)
XLA Ops:
  7.2 0.0 copy-start
  7.2 0.0 copy-start.3
  7.2 0.0 reduce-scatter.6.cloned.1.call-start
  7.2 3.9 convolution_bitcast_fusion.1
  11.1 0.0 copy-done.3
  11.1 0.0 copy-start.4
  11.1 4.0 fusion.12
  15.1 0.0 reduce-scatter.6.cloned.1.call-update
  15.2 0.0 copy-start.2
  15.2 0.0 reduce-scatter.8.cloned.1.call-start
  15.2 0.0 copy-done
  15.2 0.0 copy-done.4
  15.3 1.1 fusion.9
  16.4 3.5 convolution_bitcast_fusion
  19.8 0.0 copy-start.1
  19.8 2.0 copy-done.1
  21.8 0.0 copy-done.2
  21.8 6.6 convolution_multiply_fusion
  28.4 0.0 reduce-scatter.8.cloned.1.call-update
  28.4 5.2 fusion.16
  33.6 158.2 %reduce-scatter.6.cloned.1.call-done = f32[192,5,16]{0,2,1:T(8,128)} async-done(((f32[192,40,16]{0,2,1:T(8,128)}), f32[192,5,16]{0,2,1:T(8,128)}) %reduce-scatter.6.cloned.1.call-update) | async-done | bytes 61456 | tf_op jit(solution)/shard_map/reduce_scatter | solution.py:24
  191.8 1.5 fusion.15
  193.3 0.2 copy.12
  193.5 0.9 copy.15
  194.3 1464.1 %reduce-scatter.8.cloned.1.call-done = f32[40,384]{1,0:T(8,128)} async-done(((f32[5120,384]{1,0:T(8,128)}), f32[40,384]{1,0:T(8,128)}) %reduce-scatter.8.cloned.1.call-update) | async-done | bytes 61456
Async XLA Ops:
  7.2 8.1 copy-start
  7.2 3.9 copy-start.3
  7.2 184.6 %reduce-scatter.6.cloned.1.call-start = ((), (), s32[]{:S(2)}) async-start(), calls=%async_computation.2 | async-start | bytes 737280 | tf_op jit(solution)/shard_map/reduce_scatter | solution.py:24
  11.1 4.1 copy-start.4
  15.2 6.6 copy-start.2
  15.2 1643.3 %reduce-scatter.8.cloned.1.call-start = ((), (), s32[]{:S(2)}) async-start(), calls=%async_computation.3 | async-start | bytes 7925760
  19.8 2.0 copy-start.1
Sparse Core Ops, SparseCore 0:
  15.3 176.4 reduce-scatter.5
  195.8 1462.6 reduce-scatter.7
where the time goes:
time: 1680 us; the launch traced here: 1670 us
  waiting for transfers between devices  1620 us (96%)
  matrix products  25.7 us (2%)
    unnamed x3, waiting for transfers between devices  1460 us
    reduce_scatter x1, waiting for transfers between devices, shards(): own_code = lax.psum_scatter(code, 'mp', scatter_dimension=1, tiled=True)  158 us
  transfers between devices with their start and end apart: 2, of which 2 were waited for; matrix products, arithmetic and copies ran while one was open for 1% of the time, Pallas kernels for 0%

commit v1 on v0

v1 whole, which is shorter than its diff:
```python
import functools

import jax
import jax.numpy as jnp
from jax import lax
from jax.experimental import pallas as pl
from jax.experimental.pallas import tpu as pltpu
from jax.sharding import PartitionSpec as P

MESH = pl.DeviceIdType.MESH
F32 = jnp.float32
BF16 = jnp.bfloat16
NN = (((1,), (0,)), ((), ()))
NT = (((1,), (1,)), ((), ()))
TN = (((0,), (0,)), ((), ()))


def dot(a, b, dims):
    return lax.dot_general(a, b, dims, preferred_element_type=F32)


def diagonal(blocks):
    zero = jnp.zeros_like(blocks[0])
    rows = [
        jnp.concatenate([b if i == j else zero for j in range(len(blocks))], axis=1)
        for i, b in enumerate(blocks)
    ]
    return jnp.concatenate(rows, axis=0)


def split(value):
    high = value.astype(BF16).astype(F32)
    return high, value - high


def kernel(
    scale,
    attn_hbm, w_hbm, enc_hbm, dec_hbm, cot_hbm,
    mixed_out, gattn_out, gw_out,
    attn, w, enc, dec, cot,
    w2, chi, clo, term, core_in, y_in, summed, z1_in, quad, z2a_in, z2b_in, pair, whole,
    blk, x_in, zsum, relay_in, far_in, dmain, dtail_a, dtail_b,
    mixed, gattn, gw_rows, gw,
    in_sem, w_sem, cot_sem, out_sem, know8,
    core_s, core_r, y_s, y_r, x_s, x_r, z1_s, z1_r, z2a_s, z2a_r, z2b_s, z2b_r,
    fin_s, fin_r, rel_s, rel_r, far_s, far_r,
):
    dp = lax.axis_index("dp")
    mp = lax.axis_index("mp")
    core = dp % 2
    zl = (dp // 2) % 16
    y = dp // 32
    x = mp // 2
    zh = mp % 2
    z = zh * 16 + zl
    a = zl // 4
    b = zl % 4
    q = a % 2
    half = a // 2
    j = zl % 8

    def along_z(step):
        to = (z + step + 32) % 32
        return ((y * 16 + to % 16) * 2 + core, x * 2 + to // 16)

    other_core = (dp + 1 - 2 * core, mp)
    x_ids = [(dp, ((x + d) % 4) * 2 + zh) for d in (1, 2, 3)]
    y_ids = [((((y + d) % 4) * 16 + zl) * 2 + core, mp) for d in (1, 2, 3)]
    quad_ids = [((y * 16 + a * 4 + (b + d) % 4) * 2 + core, mp) for d in (1, 2, 3)]
    z4_id = ((y * 16 + zl + 4 - 8 * q) * 2 + core, mp)
    z8_id = ((y * 16 + zl + 8 - 16 * half) * 2 + core, mp)

    def remote(src, dst, send, recv, to):
        return pltpu.make_async_remote_copy(
            src_ref=src, dst_ref=dst, send_sem=send, recv_sem=recv,
            device_id=to, device_id_type=MESH,
        )

    barrier = pltpu.get_barrier_semaphore()
    near = [other_core] + x_ids + y_ids + quad_ids + [along_z(4), along_z(-4)]
    for to in near:
        pl.semaphore_signal(barrier, inc=1, device_id=to, device_id_type=MESH)

    attn_copy = pltpu.make_async_copy(attn_hbm, attn, in_sem.at[0])
    dec_copy = pltpu.make_async_copy(dec_hbm, dec, in_sem.at[1])
    enc_copy = pltpu.make_async_copy(enc_hbm, enc, in_sem.at[2])
    dec_copy.start()
    attn_copy.start()
    cot_order = [2 * i + 1 - core for i in range(4)] + [2 * i + core for i in range(4)]
    cot_copies = []
    for i, m in enumerate(cot_order):
        cols = pl.ds(pl.multiple_of(m * 640, 128), 640)
        copy = pltpu.make_async_copy(cot_hbm.at[:, cols], cot.at[i], cot_sem.at[i])
        copy.start()
        cot_copies.append(copy)
    enc_copy.start()
    w_order = [(((x + d) % 4) * 2 + 1 - zh) for d in (1, 2, 3, 0)]
    w_order += [(((x + d) % 4) * 2 + zh) for d in (1, 2, 3, 0)]
    w_copies = []
    for i, m in enumerate(w_order):
        rows = pl.ds(pl.multiple_of(m * 640, 128), 640)
        copy = pltpu.make_async_copy(w_hbm.at[rows, :], w.at[i], w_sem.at[i])
        copy.start()
        w_copies.append(copy)

    dec_copy.wait()
    attn_copy.wait()
    attn_v = attn[...]
    for i, m in enumerate(cot_order):
        cot_copies[i].wait()
        d_block = diagonal([dec[m * 5 + g] for g in range(5)])
        coded = dot(d_block, cot[i], NT)
        high, low = split(coded)
        high = high.astype(BF16)
        chi[m] = high
        clo[m] = low.astype(BF16)
        term[m] = dot(high, attn_v, NN)

    pl.semaphore_wait(barrier, len(near))
    for to in (along_z(4), along_z(-4)):
        pl.semaphore_signal(know8, inc=1, device_id=to, device_id_type=MESH)

    core_copies = []
    for d in (1, 2, 3, 0):
        yy = (y + d) % 4
        copy = remote(
            term.at[2 * yy + 1 - core], core_in.at[yy], core_s.at[d], core_r.at[d], other_core
        )
        copy.start()
        core_copies.append(copy)

    enc_copy.wait()

    def code_blocks(side):
        copies = []
        for i, d in enumerate((1, 2, 3, 0)):
            m = w_order[side * 4 + i]
            w_copies[side * 4 + i].wait()
            e_block = diagonal([enc[m * 5 + g] for g in range(5)])
            w2_block = dot(e_block, w[side * 4 + i], NN).astype(BF16)
            w2[m] = w2_block
            code = dot(w2_block, attn_v, NT)
            to = (x + d) % 4
            blk[side, to, 0:80, :] = code[:, 0:128]
            blk[side, to, 80:120, :] = jnp.concatenate(
                [code[0:40, 128:192], code[40:80, 128:192]], axis=1
            )
            if d:
                copy = remote(
                    blk.at[side, to], x_in.at[side, d - 1],
                    x_s.at[side, d - 1], x_r.at[side, d - 1], x_ids[d - 1],
                )
                copy.start()
                copies.append(copy)
        return copies

    away_copies = code_blocks(0)

    y_copies = []
    for i, d in enumerate((1, 2, 3, 0)):
        yy = (y + d) % 4
        core_copies[i].wait_recv()
        core_in[yy] = core_in[yy] + term[2 * yy + core]
        if d:
            copy = remote(
                core_in.at[yy], y_in.at[d - 1], y_s.at[d - 1], y_r.at[d - 1], y_ids[d - 1]
            )
            copy.start()
            y_copies.append(copy)

    own_copies = code_blocks(1)

    for copy in away_copies:
        copy.wait_recv()
    zsum[...] = blk[0, x] + x_in[0, 0] + x_in[0, 1] + x_in[0, 2]
    pl.semaphore_wait(know8, 2)
    up, down = pl.ds(0, 64), pl.ds(64, 56)
    relays = [
        remote(zsum.at[up], relay_in.at[up], rel_s.at[0], rel_r.at[0], along_z(8)),
        remote(zsum.at[down], relay_in.at[down], rel_s.at[1], rel_r.at[1], along_z(-8)),
    ]
    for copy in relays:
        copy.start()

    for copy in y_copies:
        copy.wait_recv()
    summed[...] = (core_in[y] + y_in[0] + y_in[1] + y_in[2]).reshape(5, 16, 384)

    def needed(at):
        return (at // 2, 2 - at % 2 + at // 2, 3 + at // 2)

    z1_copies = []
    for d in (1, 2, 3):
        for s, group in enumerate(needed((b + d) % 4)):
            copy = remote(
                summed.at[group], z1_in.at[d - 1, s],
                z1_s.at[d - 1, s], z1_r.at[d - 1, s], quad_ids[d - 1],
            )
            copy.start()
            z1_copies.append(copy)

    d_own = diagonal([dec[mp * 5 + g] for g in range(5)]).astype(F32)
    dmain[...] = jnp.concatenate([d_own, d_own], axis=0).astype(BF16)
    dtail_a[...] = jnp.concatenate([d_own[0:40], d_own[0:40]], axis=0).astype(BF16)
    dtail_b[...] = jnp.concatenate([d_own[40:80], d_own[40:80]], axis=0).astype(BF16)

    w2_v = w2[...].reshape(640, 384)
    grad = dot(chi[...].reshape(640, 192), w2_v, TN)
    grad = grad + dot(clo[...].reshape(640, 192), w2_v, TN)
    gattn[...] = grad.astype(BF16)
    gattn_copy = pltpu.make_async_copy(gattn, gattn_out, out_sem.at[0])
    gattn_copy.start()

    for copy in relays:
        copy.wait_recv()
    fars = [
        remote(relay_in.at[up], far_in.at[up], far_s.at[0], far_r.at[0], along_z(8)),
        remote(relay_in.at[down], far_in.at[down], far_s.at[1], far_r.at[1], along_z(-8)),
    ]
    for copy in fars:
        copy.start()

    for copy in z1_copies:
        copy.wait_recv()
    for s, group in enumerate(needed(b)):
        quad[s] = summed[group] + z1_in[0, s] + z1_in[1, s] + z1_in[2, s]
    z2a = remote(quad.at[pl.ds(1 - q, 2)], z2a_in, z2a_s, z2a_r, z4_id)
    z2a.start()

    for copy in own_copies:
        copy.wait_recv()
    code_near = blk[1, x] + x_in[1, 0] + x_in[1, 1] + x_in[1, 2]

    z2a.wait_recv()
    pair[...] = quad[pl.ds(q, 2)] + z2a_in[...]
    z2b = remote(pair, z2b_in, z2b_s, z2b_r, z8_id)
    fin = remote(whole, whole, fin_s, fin_r, other_core)

    @pl.when(half != core)
    def _():
        z2b.start()

    for copy in fars:
        copy.wait_recv()
    code_sum = code_near + far_in[...]
    high, low = split(code_sum)
    main = jnp.concatenate([high[0:80], low[0:80]], axis=0).astype(BF16)
    tail = jnp.concatenate([high[80:120], low[80:120]], axis=0).astype(BF16)
    mixed[0:128, :] = dot(main, dmain[...], TN).astype(BF16)
    tail_a = dot(tail, dtail_a[...], TN)
    tail_b = dot(tail, dtail_b[...], TN)
    mixed[128:192, :] = (tail_a[0:64] + tail_b[64:128]).astype(BF16)
    mixed_copy = pltpu.make_async_copy(mixed, mixed_out, out_sem.at[1])
    mixed_copy.start()

    @pl.when(half == core)
    def _():
        z2b.wait_recv()
        whole[...] = pair[...] + z2b_in[...]
        fin.start()

    @pl.when(half != core)
    def _():
        fin.wait_recv()

    groups = needed(b)
    first = groups[0] * (1 - q) + groups[1] * q
    second = groups[1] * (1 - q) + groups[2] * q
    base = (2 * y + half) * 5
    e_pair = diagonal([enc[base + first], enc[base + second]])
    g_high, g_low = split(whole[...].reshape(32, 384))
    g_both = jnp.concatenate([g_high, g_low], axis=0).astype(BF16)
    e_both = jnp.concatenate([e_pair, e_pair], axis=0)
    gw_rows[...] = dot(e_both, g_both, TN) * scale
    jump = (b % 2) * q
    start = 40 * (2 * j + core) - 128 * (first * (1 - jump) + (second - 1) * jump)
    gw[...] = gw_rows[pl.ds(pl.multiple_of(start, 8), 40), :]
    gw_copy = pltpu.make_async_copy(gw, gw_out, out_sem.at[2])
    gw_copy.start()

    for copy in core_copies + away_copies + y_copies + own_copies + relays + fars + z1_copies:
        copy.wait_send()
    z2a.wait_send()

    @pl.when(half != core)
    def _():
        z2b.wait_send()

    @pl.when(half == core)
    def _():
        fin.wait_send()

    gattn_copy.wait()
    mixed_copy.wait()
    gw_copy.wait()


def solution(mesh):
    dp_count = mesh.shape["dp"]

    def shards(attn, w_out, encoder, decoder, cotangent):
        scale = float(attn.shape[0] * dp_count) ** (-0.5)
        enc_t = jnp.transpose(encoder, (0, 2, 1))
        anywhere = pl.BlockSpec(memory_space=pl.ANY)
        dma = pltpu.SemaphoreType.DMA
        vmem = pltpu.VMEM
        return pl.pallas_call(
            functools.partial(kernel, scale),
            out_shape=(
                jax.ShapeDtypeStruct((192, 640), BF16),
                jax.ShapeDtypeStruct((192, 384), BF16),
                jax.ShapeDtypeStruct((40, 384), F32),
            ),
            in_specs=[anywhere] * 5,
            out_specs=(anywhere,) * 3,
            scratch_shapes=[
                vmem((192, 384), BF16),
                vmem((8, 640, 384), BF16),
                vmem((40, 16, 128), BF16),
                vmem((40, 16, 128), BF16),
                vmem((8, 192, 640), BF16),
                vmem((8, 80, 384), BF16),
                vmem((8, 80, 192), BF16),
                vmem((8, 80, 192), BF16),
                vmem((8, 80, 384), F32),
                vmem((4, 80, 384), F32),
                vmem((3, 80, 384), F32),
                vmem((5, 16, 384), F32),
                vmem((3, 3, 16, 384), F32),
                vmem((3, 16, 384), F32),
                vmem((2, 16, 384), F32),
                vmem((2, 16, 384), F32),
                vmem((2, 16, 384), F32),
                vmem((2, 16, 384), F32),
                vmem((2, 4, 120, 128), F32),
                vmem((2, 3, 120, 128), F32),
                vmem((120, 128), F32),
                vmem((120, 128), F32),
                vmem((120, 128), F32),
                vmem((160, 640), BF16),
                vmem((80, 640), BF16),
                vmem((80, 640), BF16),
                vmem((192, 640), BF16),
                vmem((192, 384), BF16),
                vmem((256, 384), F32),
                vmem((40, 384), F32),
                dma((3,)), dma((8,)), dma((8,)), dma((3,)),
                pltpu.SemaphoreType.REGULAR,
                dma((4,)), dma((4,)),
                dma((3,)), dma((3,)),
                dma((2, 3)), dma((2, 3)),
                dma((3, 3)), dma((3, 3)),
                dma, dma,
                dma, dma,
                dma, dma,
                dma((2,)), dma((2,)),
                dma((2,)), dma((2,)),
            ],
            compiler_params=pltpu.CompilerParams(
                collective_id=0, has_side_effects=True, vmem_limit_bytes=48 * 1024 * 1024
            ),
            name="coded_projection",
        )(attn, w_out, enc_t, decoder, cotangent)

    return jax.shard_map(
        shards,
        mesh=mesh,
        in_specs=(P("dp", "mp"), P(None, "mp"), P(), P(), P("dp", None)),
        out_specs=(P("dp", "mp"), P("dp", "mp"), P("dp", "mp")),
        check_vma=False,
    )
```

time: 1680 us -> 70.4 us (0.04)
  waiting for transfers between devices: 1620 us -> 0 us
  Pallas kernels: 0 us -> 63.3 us
  matrix products: 25.7 us -> 0 us
    unnamed x3 -> x0, waiting for transfers between devices: 1460 us -> none
    reduce_scatter x1 -> x0, waiting for transfers between devices: 158 us -> none  [shards(): own_code = lax.psum_scatter(code, 'mp', scatter_dimension=1, tiled=True)]
    pallas_call x0 -> x1, Pallas kernels: none -> 63.3 us  [shards(): pl.pallas_call(functools.partial(kernel, scale), out_shape=(jax.ShapeDtyp...]
    dot_general x7 -> x0, matrix products: 25.7 us -> none  [the longest x1 6.56 us: shards(): jnp.dot(spread.T, attn_float, precision=high) * scale]
  transfers between devices with their start and end apart: 2 -> 0, of which waited for: 2 -> 0; matrix products, arithmetic and copies ran while one was open for 1% -> 0% of each run, Pallas kernels for 0% -> 0%
where the time goes in v1:
time: 70.4 us; the launch traced here: 70.2 us
  Pallas kernels  63.3 us (90%)
  local copies, waits for them, and re-layouts  6.26 us (9%)
    pallas_call x1, Pallas kernels, shards(): pl.pallas_call(functools.partial(kernel, scale), out_shape=(jax.ShapeDtyp...  63.3 us
    unnamed x11, local copies, waits for them, and re-layouts  6.26 us

profile of v1, /device:TPU:7, one launch (start us, length us, event | category | flops | bytes accessed | tf_op | source)
XLA Modules:
  0.0 70.2 jit_solution(17790645633655029960)
XLA Ops:
  0.6 0.0 copy-start
  0.6 1.5 %copy-done = bf16[192,5120]{1,0:T(8,128)(2,1)S(1)} copy-done((bf16[192,5120]{1,0:T(8,128)(2,1)S(1)}, bf16[192,5120]{1,0:T(8,128)(2,1)}, u32[]{:S(2)}) %copy-start) | copy-done | bytes 1966104
  2.2 0.0 copy-start.1
  2.2 0.9 %copy-done.1 = bf16[40,128,16]{1,2,0:T(8,128)(2,1)S(1)} copy-done((bf16[40,128,16]{1,2,0:T(8,128)(2,1)S(1)}, bf16[40,128,16]{1,2,0:T(8,128)(2,1)}, u32[]{:S(2)}) %copy-start.1) | copy-done | bytes 163864
  3.1 0.0 copy-start.2
  3.1 0.9 %copy-done.2 = bf16[40,16,128]{2,1,0:T(8,128)(2,1)S(1)} copy-done((bf16[40,16,128]{2,1,0:T(8,128)(2,1)S(1)}, bf16[40,16,128]{2,1,0:T(8,128)(2,1)}, u32[]{:S(2)}) %copy-start.2) | copy-done | bytes 163864
  4.0 0.0 copy-start.3
  4.0 0.9 %copy-done.3 = bf16[192,384]{1,0:T(8,128)(2,1)S(1)} copy-done((bf16[192,384]{1,0:T(8,128)(2,1)S(1)}, bf16[192,384]{1,0:T(8,128)(2,1)}, u32[]{:S(2)}) %copy-start.3) | copy-done | bytes 147480
  4.9 63.3 %coded_projection.1 = (bf16[192,640]{1,0:T(8,128)(2,1)S(1)}, bf16[192,384]{1,0:T(8,128)(2,1)S(1)}, f32[40,384]{1,0:T(8,128)S(1)}) custom-call(bf16[192,384]{1,0:T(8,128)(2,1)S(1)} %copy-done.3, bf16[5120,384]{1,0:T(8,128)(2,1)} %w_hbm.1, bf16[40,16,128]{2,1,0:T(8,128)(2,1)S(1)} %bitcast.1, bf16[40,16,128]{2,1,0:T(8,128)(2,1)S(1)} %copy-done.2, ...), custom_call_target="tpu_custom_call" | custom-call | tf_op jit(solution)/shard_map/coded_projection/pallas_call | solution.py:307
  68.2 0.7 copy.11
  68.9 0.7 copy.12
  69.6 0.6 copy.13
Async XLA Ops:
  0.6 1.5 %copy-start = (bf16[192,5120]{1,0:T(8,128)(2,1)S(1)}, bf16[192,5120]{1,0:T(8,128)(2,1)}, u32[]{:S(2)}) copy-start(bf16[192,5120]{1,0:T(8,128)(2,1)} %cot_hbm.1) | copy-start | bytes 5898244
  2.2 0.9 %copy-start.1 = (bf16[40,128,16]{1,2,0:T(8,128)(2,1)S(1)}, bf16[40,128,16]{1,2,0:T(8,128)(2,1)}, u32[]{:S(2)}) copy-start(bf16[40,128,16]{1,2,0:T(8,128)(2,1)} %param.7) | copy-start | bytes 491524
  3.1 0.9 %copy-start.2 = (bf16[40,16,128]{2,1,0:T(8,128)(2,1)S(1)}, bf16[40,16,128]{2,1,0:T(8,128)(2,1)}, u32[]{:S(2)}) copy-start(bf16[40,16,128]{2,1,0:T(8,128)(2,1)} %dec_hbm.1) | copy-start | bytes 491524
  4.0 0.9 %copy-start.3 = (bf16[192,384]{1,0:T(8,128)(2,1)S(1)}, bf16[192,384]{1,0:T(8,128)(2,1)}, u32[]{:S(2)}) copy-start(bf16[192,384]{1,0:T(8,128)(2,1)} %attn_hbm.1) | copy-start | bytes 442372

commit v2 on v1

v2 whole, which is shorter than its diff:
```python
import functools

import jax
import jax.numpy as jnp
from jax import lax
from jax.experimental import pallas as pl
from jax.experimental.pallas import tpu as pltpu
from jax.sharding import PartitionSpec as P

MESH = pl.DeviceIdType.MESH
CUTS = 3
F32 = jnp.float32
BF16 = jnp.bfloat16
NN = (((1,), (0,)), ((), ()))
NT = (((1,), (1,)), ((), ()))
TN = (((0,), (0,)), ((), ()))


def dot(a, b, dims):
    return lax.dot_general(a, b, dims, preferred_element_type=F32)


def diagonal(blocks):
    zero = jnp.zeros_like(blocks[0])
    rows = [
        jnp.concatenate([b if i == j else zero for j in range(len(blocks))], axis=1)
        for i, b in enumerate(blocks)
    ]
    return jnp.concatenate(rows, axis=0)


def split(value):
    high = value.astype(BF16).astype(F32)
    return high, value - high


def kernel(
    scale,
    attn_hbm, w_hbm, enc_hbm, dec_hbm, cot_hbm,
    mixed_out, gattn_out, gw_out,
    attn, w, enc, dec, cot,
    w2, chi, clo, term, core_in, y_in, classes, z1_in, quad, z2a_in, z2b_in, pair, whole,
    blk, x_in, zsum, relay_in, far_in, dmain, dtail_a, dtail_b, gw_rows,
    in_sem, w_sem, cot_sem, ready8, ready16,
    core_s, core_r, y_s, y_r, x_s, x_r, z1_s, z1_r, z2a_s, z2a_r, z2b_s, z2b_r,
    fin_s, fin_r, far_s, far_r, rel_s, rel_r,
):
    dp = lax.axis_index("dp")
    mp = lax.axis_index("mp")
    core = dp % 2
    zl = (dp // 2) % 16
    y = dp // 32
    x = mp // 2
    zh = mp % 2
    a = zl // 4
    b = zl % 4
    q = a % 2
    half = a // 2
    j = zl % 8

    other_core = (dp + 1 - 2 * core, mp)
    x_ids = [(dp, ((x + d) % 4) * 2 + zh) for d in (1, 2, 3)]
    y_ids = [((((y + d) % 4) * 16 + zl) * 2 + core, mp) for d in (1, 2, 3)]
    quad_ids = [((y * 16 + a * 4 + (b + d) % 4) * 2 + core, mp) for d in (1, 2, 3)]
    z4_id = ((y * 16 + zl + 4 - 8 * q) * 2 + core, mp)
    z8_id = ((y * 16 + zl + 8 - 16 * half) * 2 + core, mp)

    def remote(src, dst, send, recv, to):
        return pltpu.make_async_remote_copy(
            src_ref=src, dst_ref=dst, send_sem=send, recv_sem=recv,
            device_id=to, device_id_type=MESH,
        )

    barrier = pltpu.get_barrier_semaphore()
    near = [other_core] + x_ids + y_ids + quad_ids + [z4_id]
    z16_id = ((y * 16 + a * 4 + (b + 2) % 4) * 2 + core, x * 2 + 1 - zh)
    for to in near:
        pl.semaphore_signal(barrier, inc=1, device_id=to, device_id_type=MESH)

    @pl.when(half == 0)
    def _():
        pl.semaphore_signal(barrier, inc=1, device_id=z8_id, device_id_type=MESH)

    @pl.when(zh == 0)
    def _():
        pl.semaphore_signal(barrier, inc=1, device_id=z16_id, device_id_type=MESH)

    attn_copy = pltpu.make_async_copy(attn_hbm, attn, in_sem.at[0])
    dec_copy = pltpu.make_async_copy(dec_hbm, dec, in_sem.at[1])
    enc_copy = pltpu.make_async_copy(enc_hbm, enc, in_sem.at[2])
    dec_copy.start()
    attn_copy.start()
    cot_order = [2 * i + 1 - core for i in range(4)] + [2 * i + core for i in range(4)]
    cot_copies = []
    for i, m in enumerate(cot_order):
        cols = pl.ds(pl.multiple_of(m * 640, 128), 640)
        copy = pltpu.make_async_copy(cot_hbm.at[:, cols], cot.at[i], cot_sem.at[i])
        copy.start()
        cot_copies.append(copy)
    enc_copy.start()
    w_order = [(((x + d) % 4) * 2 + 1 - zh) for d in (1, 2, 3, 0)]
    w_order += [(((x + d) % 4) * 2 + zh) for d in (1, 2, 3, 0)]
    w_copies = []
    for i, m in enumerate(w_order):
        rows = pl.ds(pl.multiple_of(m * 640, 128), 640)
        copy = pltpu.make_async_copy(w_hbm.at[rows, :], w.at[i], w_sem.at[i])
        copy.start()
        w_copies.append(copy)

    dec_copy.wait()
    attn_copy.wait()
    attn_v = attn[...]

    wide = 384 // CUTS

    def gradient_terms(side):
        for i in range(4):
            cot_copies[4 * side + i].wait()
        for i in range(4 * side, 4 * side + 4):
            m = cot_order[i]
            d_block = diagonal([dec[m * 5 + g] for g in range(5)])
            coded = dot(d_block, cot[i], NT)
            high, low = split(coded)
            high = high.astype(BF16)
            chi[m] = high
            clo[m] = low.astype(BF16)
            product = dot(high, attn_v, NN)
            for l in range(CUTS):
                term[l, m % 2, m // 2] = product[:, wide * l:wide * (l + 1)]

    gradient_terms(0)
    pl.semaphore_wait(barrier, len(near) + half + zh)
    core_copies = []
    for l in range(CUTS):
        copy = remote(
            term.at[l, 1 - core], core_in.at[l], core_s.at[l], core_r.at[l], other_core
        )
        copy.start()
        core_copies.append(copy)

    @pl.when(half == 1)
    def _():
        pl.semaphore_signal(ready8, inc=1, device_id=z8_id, device_id_type=MESH)

    @pl.when(zh == 1)
    def _():
        pl.semaphore_signal(ready16, inc=1, device_id=z16_id, device_id_type=MESH)

    enc_copy.wait()

    def code_blocks(side):
        for i in range(4):
            w_copies[4 * side + i].wait()
        for i in range(4):
            m = w_order[4 * side + i]
            to = m // 2
            e_block = diagonal([enc[m * 5 + g] for g in range(5)])
            w2_block = dot(e_block, w[4 * side + i], NN).astype(BF16)
            w2[m] = w2_block
            code = dot(w2_block, attn_v, NT)
            blk[side, to, 0:80, :] = code[:, 0:128]
            blk[side, to, 80:120, :] = jnp.concatenate(
                [code[0:40, 128:192], code[40:80, 128:192]], axis=1
            )
        copies = []
        for d in (1, 2, 3):
            copy = remote(
                blk.at[side, (x + d) % 4], x_in.at[side, d - 1],
                x_s.at[side, d - 1], x_r.at[side, d - 1], x_ids[d - 1],
            )
            copy.start()
            copies.append(copy)
        return copies

    away_copies = code_blocks(0)
    gradient_terms(1)

    far = remote(zsum, relay_in, far_s, far_r, z16_id)
    last = remote(relay_in, far_in, rel_s, rel_r, quad_ids[1])

    def send_away():
        for copy in away_copies:
            copy.wait_recv()
        zsum[...] = blk[0, x] + x_in[0, 0] + x_in[0, 1] + x_in[0, 2]
        far.start()

    @pl.when(zh == 1)
    def _():
        send_away()

    y_copies = [[] for _ in range(CUTS)]
    for l in range(CUTS):
        core_copies[l].wait_recv()
        for d in (1, 2, 3, 0):
            yy = (y + d) % 4
            core_in[l, yy] = core_in[l, yy] + term[l, core, yy]
            if d:
                copy = remote(
                    core_in.at[l, yy], y_in.at[l, d - 1],
                    y_s.at[l, d - 1], y_r.at[l, d - 1], y_ids[d - 1],
                )
                copy.start()
                y_copies[l].append(copy)

    own_copies = code_blocks(1)

    def needed(at):
        return (at // 2, 2 - at % 2 + at // 2, 3 + at // 2)

    z1_copies = [[] for _ in range(CUTS)]
    for l in range(CUTS):
        for copy in y_copies[l]:
            copy.wait_recv()
        total = core_in[l, y] + y_in[l, 0] + y_in[l, 1] + y_in[l, 2]
        total = total.reshape(5, 16, wide)
        for at in range(4):
            for s, group in enumerate(needed(at)):
                classes[l, at, s] = total[group]
        for d in (1, 2, 3):
            copy = remote(
                classes.at[l, (b + d) % 4], z1_in.at[l, d - 1],
                z1_s.at[l, d - 1], z1_r.at[l, d - 1], quad_ids[d - 1],
            )
            copy.start()
            z1_copies[l].append(copy)

    d_own = diagonal([dec[mp * 5 + g] for g in range(5)]).astype(F32)
    dmain[...] = jnp.concatenate([d_own, d_own], axis=0).astype(BF16)
    dtail_a[...] = jnp.concatenate([d_own[0:40], d_own[0:40]], axis=0).astype(BF16)
    dtail_b[...] = jnp.concatenate([d_own[40:80], d_own[40:80]], axis=0).astype(BF16)

    w2_v = w2[...].reshape(640, 384)
    grad = dot(chi[...].reshape(640, 192), w2_v, TN)
    grad = grad + dot(clo[...].reshape(640, 192), w2_v, TN)
    gattn_out[...] = grad.astype(BF16)

    single = b % 2 == q
    z2a_copies = []
    for l in range(CUTS):
        for copy in z1_copies[l]:
            copy.wait_recv()
        quad[l] = classes[l, b] + z1_in[l, 0] + z1_in[l, 1] + z1_in[l, 2]
        two = remote(
            quad.at[l, pl.ds(1 - q, 2)], z2a_in.at[l], z2a_s.at[l], z2a_r.at[l], z4_id
        )
        one = remote(
            quad.at[l, pl.ds(2 - 2 * q, 1)], z2a_in.at[l, pl.ds(1 - q, 1)],
            z2a_s.at[l], z2a_r.at[l], z4_id,
        )
        z2a_copies.append((one, two))

        @pl.when(single)
        def _(two=two):
            two.start()

        @pl.when(jnp.logical_not(single))
        def _(one=one):
            one.start()

    for copy in own_copies:
        copy.wait_recv()
    code_near = blk[1, x] + x_in[1, 0] + x_in[1, 1] + x_in[1, 2]

    @pl.when(half == 0)
    def _():
        pl.semaphore_wait(ready8, 1)

    z2b_copies = [
        (
            remote(
                pair.at[l, pl.ds(q, 1)], z2b_in.at[l, pl.ds(q, 1)],
                z2b_s.at[l], z2b_r.at[l], z8_id,
            ),
            remote(pair.at[l], z2b_in.at[l], z2b_s.at[l], z2b_r.at[l], z8_id),
        )
        for l in range(CUTS)
    ]
    fin_copies = [
        remote(whole.at[l], whole.at[l], fin_s.at[l], fin_r.at[l], other_core) for l in range(CUTS)
    ]
    for l in range(CUTS):
        pair[l] = quad[l, pl.ds(q, 2)]

        @pl.when(single)
        def _(l=l):
            z2a_copies[l][0].wait_recv()
            pair[l, q] = pair[l, q] + z2a_in[l, q]

            @pl.when(half != core)
            def _():
                z2b_copies[l][0].start()

        @pl.when(jnp.logical_not(single))
        def _(l=l):
            z2a_copies[l][1].wait_recv()
            pair[l] = pair[l] + z2a_in[l]

            @pl.when(half != core)
            def _():
                z2b_copies[l][1].start()

    @pl.when(zh == 0)
    def _():
        pl.semaphore_wait(ready16, 1)
        send_away()

    far.wait_recv()
    last.start()

    @pl.when(half == core)
    def _():
        for l in range(CUTS):
            whole[l] = pair[l]

            @pl.when(single)
            def _(l=l):
                z2b_copies[l][0].wait_recv()
                whole[l, q] = whole[l, q] + z2b_in[l, q]

            @pl.when(jnp.logical_not(single))
            def _(l=l):
                z2b_copies[l][1].wait_recv()
                whole[l] = whole[l] + z2b_in[l]

            fin_copies[l].start()

    last.wait_recv()
    code_sum = code_near + far_in[...]
    high, low = split(code_sum)
    main = jnp.concatenate([high[0:80], low[0:80]], axis=0).astype(BF16)
    tail = jnp.concatenate([high[80:120], low[80:120]], axis=0).astype(BF16)
    mixed_out[0:128, :] = dot(main, dmain[...], TN).astype(BF16)
    tail_a = dot(tail, dtail_a[...], TN)
    tail_b = dot(tail, dtail_b[...], TN)
    mixed_out[128:192, :] = (tail_a[0:64] + tail_b[64:128]).astype(BF16)

    groups = needed(b)
    first = groups[0] * (1 - q) + groups[1] * q
    second = groups[1] * (1 - q) + groups[2] * q
    base = (2 * y + half) * 5
    e_pair = diagonal([enc[base + first], enc[base + second]])
    e_both = jnp.concatenate([e_pair, e_pair], axis=0)

    @pl.when(half != core)
    def _():
        for l in range(CUTS):
            fin_copies[l].wait_recv()

    for l in range(CUTS):
        g_high, g_low = split(whole[l].reshape(32, wide))
        g_both = jnp.concatenate([g_high, g_low], axis=0).astype(BF16)
        gw_rows[:, wide * l:wide * (l + 1)] = dot(e_both, g_both, TN) * scale
    jump = (b % 2) * q
    start = 40 * (2 * j + core) - 128 * (first * (1 - jump) + (second - 1) * jump)
    gw_out[...] = gw_rows[pl.ds(pl.multiple_of(start, 8), 40), :]

    for copy in core_copies + away_copies + own_copies + [far, last]:
        copy.wait_send()
    for l in range(CUTS):
        for copy in y_copies[l] + z1_copies[l]:
            copy.wait_send()

    for pick, want in ((0, single), (1, jnp.logical_not(single))):
        @pl.when(want)
        def _(pick=pick):
            for l in range(CUTS):
                z2a_copies[l][1 - pick].wait_send()

                @pl.when(half != core)
                def _(l=l):
                    z2b_copies[l][pick].wait_send()

    @pl.when(half == core)
    def _():
        for l in range(CUTS):
            fin_copies[l].wait_send()


def finish(mixed, gattn, gw, mixed_out, gattn_out, gw_out, sem):
    copies = [
        pltpu.make_async_copy(mixed, mixed_out, sem.at[0]),
        pltpu.make_async_copy(gattn, gattn_out, sem.at[1]),
        pltpu.make_async_copy(gw, gw_out, sem.at[2]),
    ]
    for copy in copies:
        copy.start()
    for copy in copies:
        copy.wait()


def solution(mesh):
    dp_count = mesh.shape["dp"]

    def shards(attn, w_out, encoder, decoder, cotangent):
        scale = float(attn.shape[0] * dp_count) ** (-0.5)
        enc_t = jnp.transpose(encoder, (0, 2, 1))
        wide = 384 // CUTS
        hbm = pl.BlockSpec(memory_space=pltpu.HBM)
        near = pl.BlockSpec(memory_space=pltpu.VMEM)
        shapes = (
            jax.ShapeDtypeStruct((192, 640), BF16),
            jax.ShapeDtypeStruct((192, 384), BF16),
            jax.ShapeDtypeStruct((40, 384), F32),
        )
        dma = pltpu.SemaphoreType.DMA
        vmem = pltpu.VMEM
        results = pl.pallas_call(
            functools.partial(kernel, scale),
            out_shape=shapes,
            in_specs=[hbm] * 5,
            out_specs=(near,) * 3,
            scratch_shapes=[
                vmem((192, 384), BF16),
                vmem((8, 640, 384), BF16),
                vmem((40, 16, 128), BF16),
                vmem((40, 16, 128), BF16),
                vmem((8, 192, 640), BF16),
                vmem((8, 80, 384), BF16),
                vmem((8, 80, 192), BF16),
                vmem((8, 80, 192), BF16),
                vmem((CUTS, 2, 4, 80, wide), F32),
                vmem((CUTS, 4, 80, wide), F32),
                vmem((CUTS, 3, 80, wide), F32),
                vmem((CUTS, 4, 3, 16, wide), F32),
                vmem((CUTS, 3, 3, 16, wide), F32),
                vmem((CUTS, 3, 16, wide), F32),
                vmem((CUTS, 2, 16, wide), F32),
                vmem((CUTS, 2, 16, wide), F32),
                vmem((CUTS, 2, 16, wide), F32),
                vmem((CUTS, 2, 16, wide), F32),
                vmem((2, 4, 120, 128), F32),
                vmem((2, 3, 120, 128), F32),
                vmem((120, 128), F32),
                vmem((120, 128), F32),
                vmem((120, 128), F32),
                vmem((160, 640), BF16),
                vmem((80, 640), BF16),
                vmem((80, 640), BF16),
                vmem((256, 384), F32),
                dma((3,)), dma((8,)), dma((8,)),
                pltpu.SemaphoreType.REGULAR, pltpu.SemaphoreType.REGULAR,
                dma((3,)), dma((3,)),
                dma((3, 3)), dma((3, 3)),
                dma((2, 3)), dma((2, 3)),
                dma((3, 3)), dma((3, 3)),
                dma((3,)), dma((3,)),
                dma((3,)), dma((3,)),
                dma((3,)), dma((3,)),
                dma, dma,
                dma, dma,
            ],
            compiler_params=pltpu.CompilerParams(
                collective_id=0, has_side_effects=True, vmem_limit_bytes=56 * 1024 * 1024
            ),
            name="coded_projection",
        )(attn, w_out, enc_t, decoder, cotangent)
        return pl.pallas_call(
            finish,
            out_shape=shapes,
            in_specs=[near] * 3,
            out_specs=(hbm,) * 3,
            scratch_shapes=[dma((3,))],
            name="finish",
        )(*results)

    return jax.shard_map(
        shards,
        mesh=mesh,
        in_specs=(P("dp", "mp"), P(None, "mp"), P(), P(), P("dp", None)),
        out_specs=(P("dp", "mp"), P("dp", "mp"), P("dp", "mp")),
        check_vma=False,
    )
```

time: 70.4 us -> 65.9 us (0.936); the launches traced: 70.2 us -> 64.6 us
  local copies, waits for them, and re-layouts: 6.26 us -> 0 us
    unnamed x11 -> x0, local copies, waits for them, and re-layouts: 6.26 us -> none
    pallas_call x1 -> x2, Pallas kernels: 63.3 us -> 64 us  [the longest x1 62.2 us: shards(): pl.pallas_call(functools.partial(kernel, scale), out_shape=shapes, in_spe...]
where the time goes in v2:
time: 65.9 us; the launch traced here: 64.6 us
  Pallas kernels  64 us (97%)
    pallas_call x1, Pallas kernels, shards(): pl.pallas_call(functools.partial(kernel, scale), out_shape=shapes, in_spe...  62.2 us
    pallas_call x1, Pallas kernels, shards(): pl.pallas_call(finish, out_shape=shapes, in_specs=[near] * 3, out_specs=(...  1.8 us

profile of v2, /device:TPU:7, one launch (start us, length us, event | category | flops | bytes accessed | tf_op | source)
XLA Modules:
  0.0 64.6 jit_solution(18088308276077346871)
XLA Ops:
  0.6 62.2 %coded_projection.1 = (bf16[192,640]{1,0:T(8,128)(2,1)}, bf16[192,384]{1,0:T(8,128)(2,1)}, f32[40,384]{1,0:T(8,128)}) custom-call(bf16[192,384]{1,0:T(8,128)(2,1)} %attn_hbm.1, bf16[5120,384]{1,0:T(8,128)(2,1)} %w_hbm.1, bf16[40,16,128]{2,1,0:T(8,128)(2,1)} %bitcast.1, bf16[40,16,128]{2,1,0:T(8,128)(2,1)} %dec_hbm.1, bf16[192,5120]{1,0:T(8,128)(2,1)} %cot_hbm.1), custom_call_target="tpu_custom_call" | custom-call | tf_op jit(solution)/shard_map/coded_projection/pallas_call | solution.py:407
  62.8 1.8 %finish.1 = (bf16[192,640]{1,0:T(8,128)(2,1)}, bf16[192,384]{1,0:T(8,128)(2,1)}, f32[40,384]{1,0:T(8,128)}) custom-call(bf16[192,640]{1,0:T(8,128)(2,1)} %get-tuple-element.6.mixed, bf16[192,384]{1,0:T(8,128)(2,1)} %get-tuple-element.7.gattn, f32[40,384]{1,0:T(8,128)} %get-tuple-element.8.gw), custom_call_target="tpu_custom_call" | custom-call | tf_op jit(solution)/shard_map/finish/pallas_call | solution.py:457

commit v3 on v2

--- a/solution.py
+++ b/solution.py
@@ -94,22 +94,28 @@
     cot_copies = []
     for i, m in enumerate(cot_order):
         cols = pl.ds(pl.multiple_of(m * 640, 128), 640)
-        copy = pltpu.make_async_copy(cot_hbm.at[:, cols], cot.at[i], cot_sem.at[i])
-        copy.start()
-        cot_copies.append(copy)
-    enc_copy.start()
+        cot_copies.append(pltpu.make_async_copy(cot_hbm.at[:, cols], cot.at[i], cot_sem.at[i]))
     w_order = [(((x + d) % 4) * 2 + 1 - zh) for d in (1, 2, 3, 0)]
     w_order += [(((x + d) % 4) * 2 + zh) for d in (1, 2, 3, 0)]
     w_copies = []
     for i, m in enumerate(w_order):
         rows = pl.ds(pl.multiple_of(m * 640, 128), 640)
-        copy = pltpu.make_async_copy(w_hbm.at[rows, :], w.at[i], w_sem.at[i])
-        copy.start()
-        w_copies.append(copy)
+        w_copies.append(pltpu.make_async_copy(w_hbm.at[rows, :], w.at[i], w_sem.at[i]))
+
+    enc_copy.start()
+
+    @pl.when(zh == 0)
+    def _():
+        for copy in cot_copies + w_copies:
+            copy.start()
+
+    @pl.when(zh == 1)
+    def _():
+        for copy in w_copies[:4] + cot_copies + w_copies[4:]:
+            copy.start()
 
     dec_copy.wait()
     attn_copy.wait()
-    attn_v = attn[...]
 
     wide = 384 // CUTS
 
@@ -124,29 +130,9 @@
             high = high.astype(BF16)
             chi[m] = high
             clo[m] = low.astype(BF16)
-            product = dot(high, attn_v, NN)
+            product = dot(high, attn[...], NN)
             for l in range(CUTS):
                 term[l, m % 2, m // 2] = product[:, wide * l:wide * (l + 1)]
-
-    gradient_terms(0)
-    pl.semaphore_wait(barrier, len(near) + half + zh)
-    core_copies = []
-    for l in range(CUTS):
-        copy = remote(
-            term.at[l, 1 - core], core_in.at[l], core_s.at[l], core_r.at[l], other_core
-        )
-        copy.start()
-        core_copies.append(copy)
-
-    @pl.when(half == 1)
-    def _():
-        pl.semaphore_signal(ready8, inc=1, device_id=z8_id, device_id_type=MESH)
-
-    @pl.when(zh == 1)
-    def _():
-        pl.semaphore_signal(ready16, inc=1, device_id=z16_id, device_id_type=MESH)
-
-    enc_copy.wait()
 
     def code_blocks(side):
         for i in range(4):
@@ -157,32 +143,71 @@
             e_block = diagonal([enc[m * 5 + g] for g in range(5)])
             w2_block = dot(e_block, w[4 * side + i], NN).astype(BF16)
             w2[m] = w2_block
-            code = dot(w2_block, attn_v, NT)
+            code = dot(w2_block, attn[...], NT)
             blk[side, to, 0:80, :] = code[:, 0:128]
             blk[side, to, 80:120, :] = jnp.concatenate(
                 [code[0:40, 128:192], code[40:80, 128:192]], axis=1
             )
-        copies = []
-        for d in (1, 2, 3):
-            copy = remote(
+
+    away_copies, own_copies = [
+        [
+            remote(
                 blk.at[side, (x + d) % 4], x_in.at[side, d - 1],
                 x_s.at[side, d - 1], x_r.at[side, d - 1], x_ids[d - 1],
             )
+            for d in (1, 2, 3)
+        ]
+        for side in (0, 1)
+    ]
+
+    enc_copy.wait()
+
+    @pl.when(zh == 0)
+    def _():
+        gradient_terms(0)
+
+    @pl.when(zh == 1)
+    def _():
+        code_blocks(0)
+
+    pl.semaphore_wait(barrier, len(near) + half + zh)
+
+    @pl.when(zh == 1)
+    def _():
+        for copy in away_copies:
             copy.start()
-            copies.append(copy)
-        return copies
-
-    away_copies = code_blocks(0)
+        gradient_terms(0)
+
+    core_copies = []
+    for l in range(CUTS):
+        copy = remote(
+            term.at[l, 1 - core], core_in.at[l], core_s.at[l], core_r.at[l], other_core
+        )
+        copy.start()
+        core_copies.append(copy)
+
+    @pl.when(half == 1)
+    def _():
+        pl.semaphore_signal(ready8, inc=1, device_id=z8_id, device_id_type=MESH)
+
+    @pl.when(zh == 1)
+    def _():
+        pl.semaphore_signal(ready16, inc=1, device_id=z16_id, device_id_type=MESH)
+
     gradient_terms(1)
 
-    far = remote(zsum, relay_in, far_s, far_r, z16_id)
+    pieces = [pl.ds(0, 32), pl.ds(32, 32), pl.ds(64, 32), pl.ds(96, 24)]
+    fars = [
+        remote(zsum.at[piece], relay_in.at[piece], far_s.at[i], far_r.at[i], z16_id)
+        for i, piece in enumerate(pieces)
+    ]
     last = remote(relay_in, far_in, rel_s, rel_r, quad_ids[1])
 
     def send_away():
         for copy in away_copies:
             copy.wait_recv()
         zsum[...] = blk[0, x] + x_in[0, 0] + x_in[0, 1] + x_in[0, 2]
-        far.start()
+        fars[0].start()
 
     @pl.when(zh == 1)
     def _():
@@ -202,7 +227,24 @@
                 copy.start()
                 y_copies[l].append(copy)
 
-    own_copies = code_blocks(1)
+    @pl.when(zh == 1)
+    def _():
+        fars[1].start()
+
+    @pl.when(zh == 0)
+    def _():
+        code_blocks(0)
+        for copy in away_copies:
+            copy.start()
+
+    code_blocks(1)
+    for copy in own_copies:
+        copy.start()
+
+    @pl.when(zh == 1)
+    def _():
+        fars[2].start()
+
 
     def needed(at):
         return (at // 2, 2 - at % 2 + at // 2, 3 + at // 2)
@@ -224,6 +266,10 @@
             copy.start()
             z1_copies[l].append(copy)
 
+    @pl.when(zh == 1)
+    def _():
+        fars[3].start()
+
     d_own = diagonal([dec[mp * 5 + g] for g in range(5)]).astype(F32)
     dmain[...] = jnp.concatenate([d_own, d_own], axis=0).astype(BF16)
     dtail_a[...] = jnp.concatenate([d_own[0:40], d_own[0:40]], axis=0).astype(BF16)
@@ -303,8 +349,11 @@
     def _():
         pl.semaphore_wait(ready16, 1)
         send_away()
-
-    far.wait_recv()
+        for copy in fars[1:]:
+            copy.start()
+
+    for copy in fars:
+        copy.wait_recv()
     last.start()
 
     @pl.when(half == core)
@@ -354,7 +403,7 @@
     start = 40 * (2 * j + core) - 128 * (first * (1 - jump) + (second - 1) * jump)
     gw_out[...] = gw_rows[pl.ds(pl.multiple_of(start, 8), 40), :]
 
-    for copy in core_copies + away_copies + own_copies + [far, last]:
+    for copy in core_copies + away_copies + own_copies + fars + [last]:
         copy.wait_send()
     for l in range(CUTS):
         for copy in y_copies[l] + z1_copies[l]:
@@ -446,7 +495,7 @@
                 dma((3,)), dma((3,)),
                 dma((3,)), dma((3,)),
                 dma((3,)), dma((3,)),
-                dma, dma,
+                dma((4,)), dma((4,)),
                 dma, dma,
             ],
             compiler_params=pltpu.CompilerParams(

time: 65.9 us -> 64.1 us (0.973)
  Pallas kernels: 64 us -> 62.7 us
    pallas_call x1, Pallas kernels: 62.2 us -> 60.9 us  [shards(): pl.pallas_call(functools.partial(kernel, scale), out_shape=shapes, in_spe...]
where the time goes in v3:
time: 64.1 us; the launch traced here: 63.3 us
  Pallas kernels  62.7 us (98%)
    pallas_call x1, Pallas kernels, shards(): pl.pallas_call(functools.partial(kernel, scale), out_shape=shapes, in_spe...  60.9 us
    pallas_call x1, Pallas kernels, shards(): pl.pallas_call(finish, out_shape=shapes, in_specs=[near] * 3, out_specs=(...  1.8 us

profile of v3, /device:TPU:7, one launch (start us, length us, event | category | flops | bytes accessed | tf_op | source)
XLA Modules:
  0.0 63.3 jit_solution(6987010375827450790)
XLA Ops:
  0.6 60.9 %coded_projection.1 = (bf16[192,640]{1,0:T(8,128)(2,1)}, bf16[192,384]{1,0:T(8,128)(2,1)}, f32[40,384]{1,0:T(8,128)}) custom-call(bf16[192,384]{1,0:T(8,128)(2,1)} %attn_hbm.1, bf16[5120,384]{1,0:T(8,128)(2,1)} %w_hbm.1, bf16[40,16,128]{2,1,0:T(8,128)(2,1)} %bitcast.1, bf16[40,16,128]{2,1,0:T(8,128)(2,1)} %dec_hbm.1, bf16[192,5120]{1,0:T(8,128)(2,1)} %cot_hbm.1), custom_call_target="tpu_custom_call" | custom-call | tf_op jit(solution)/shard_map/coded_projection/pallas_call | solution.py:456
  61.5 1.8 %finish.1 = (bf16[192,640]{1,0:T(8,128)(2,1)}, bf16[192,384]{1,0:T(8,128)(2,1)}, f32[40,384]{1,0:T(8,128)}) custom-call(bf16[192,640]{1,0:T(8,128)(2,1)} %get-tuple-element.6.mixed, bf16[192,384]{1,0:T(8,128)(2,1)} %get-tuple-element.7.gattn, f32[40,384]{1,0:T(8,128)} %get-tuple-element.8.gw), custom_call_target="tpu_custom_call" | custom-call | tf_op jit(solution)/shard_map/finish/pallas_call | solution.py:506

commit v4 on v3

--- a/solution.py
+++ b/solution.py
@@ -207,7 +207,6 @@
         for copy in away_copies:
             copy.wait_recv()
         zsum[...] = blk[0, x] + x_in[0, 0] + x_in[0, 1] + x_in[0, 2]
-        fars[0].start()
 
     @pl.when(zh == 1)
     def _():
@@ -229,7 +228,7 @@
 
     @pl.when(zh == 1)
     def _():
-        fars[1].start()
+        fars[0].start()
 
     @pl.when(zh == 0)
     def _():
@@ -243,7 +242,7 @@
 
     @pl.when(zh == 1)
     def _():
-        fars[2].start()
+        fars[1].start()
 
 
     def needed(at):
@@ -268,7 +267,7 @@
 
     @pl.when(zh == 1)
     def _():
-        fars[3].start()
+        fars[2].start()
 
     d_own = diagonal([dec[mp * 5 + g] for g in range(5)]).astype(F32)
     dmain[...] = jnp.concatenate([d_own, d_own], axis=0).astype(BF16)
@@ -279,6 +278,10 @@
     grad = dot(chi[...].reshape(640, 192), w2_v, TN)
     grad = grad + dot(clo[...].reshape(640, 192), w2_v, TN)
     gattn_out[...] = grad.astype(BF16)
+
+    @pl.when(zh == 1)
+    def _():
+        fars[3].start()
 
     single = b % 2 == q
     z2a_copies = []
@@ -349,7 +352,7 @@
     def _():
         pl.semaphore_wait(ready16, 1)
         send_away()
-        for copy in fars[1:]:
+        for copy in fars:
             copy.start()
 
     for copy in fars:

time: 64.1 us -> 63.6 us (level)
  no operation moved by 1% of the time
where the time goes in v4:
time: 63.6 us; the launch traced here: 63.4 us
  Pallas kernels  62.8 us (99%)
  between operations  0.64 us (1%)
    pallas_call x1, Pallas kernels, shards(): pl.pallas_call(functools.partial(kernel, scale), out_shape=shapes, in_spe...  61 us
    pallas_call x1, Pallas kernels, shards(): pl.pallas_call(finish, out_shape=shapes, in_specs=[near] * 3, out_specs=(...  1.8 us

profile of v4, /device:TPU:7, one launch (start us, length us, event | category | flops | bytes accessed | tf_op | source)
XLA Modules:
  0.0 63.4 jit_solution(7284963084507143544)
XLA Ops:
  0.6 61.0 %coded_projection.1 = (bf16[192,640]{1,0:T(8,128)(2,1)}, bf16[192,384]{1,0:T(8,128)(2,1)}, f32[40,384]{1,0:T(8,128)}) custom-call(bf16[192,384]{1,0:T(8,128)(2,1)} %attn_hbm.1, bf16[5120,384]{1,0:T(8,128)(2,1)} %w_hbm.1, bf16[40,16,128]{2,1,0:T(8,128)(2,1)} %bitcast.1, bf16[40,16,128]{2,1,0:T(8,128)(2,1)} %dec_hbm.1, bf16[192,5120]{1,0:T(8,128)(2,1)} %cot_hbm.1), custom_call_target="tpu_custom_call" | custom-call | tf_op jit(solution)/shard_map/coded_projection/pallas_call | solution.py:459
  61.6 1.8 %finish.1 = (bf16[192,640]{1,0:T(8,128)(2,1)}, bf16[192,384]{1,0:T(8,128)(2,1)}, f32[40,384]{1,0:T(8,128)}) custom-call(bf16[192,640]{1,0:T(8,128)(2,1)} %get-tuple-element.6.mixed, bf16[192,384]{1,0:T(8,128)(2,1)} %get-tuple-element.7.gattn, f32[40,384]{1,0:T(8,128)} %get-tuple-element.8.gw), custom_call_target="tpu_custom_call" | custom-call | tf_op jit(solution)/shard_map/finish/pallas_call | solution.py:509
